TPU v7x, 128 devices: a whole 4x4x4 slice. The times are simulated.
128 devices in a mesh: row: 4 (over y), col: 32 (over z, x, core).
Axes of the slice: x: 4, y: 4, z: 4, core: 2. Of those that a mesh axis runs over, the one named last changes fastest.
Arguments:
- amplitudes: bfloat16 [8192, 4096], P('row', 'col'), may hold values from -6 to 6
- integrals: bfloat16 [4096, 32768], P('row', 'col'), may hold values from -0.09375 to 0.09375
- amp_mask: int32 [128, 64], replicated, may hold values 0 or 1
- int_mask: int32 [64, 512], replicated, may hold values 0 or 1
- pair_map: int32 [128], replicated, may hold values from 0 to 127, each once
Outputs:
- ladder: bfloat16 [8192, 32768], P('row', 'col')
All inputs are finite; a program needn't handle non-finite values.
Results may differ from a plain program's by a relative error of at most 0.0015.
Values may be sent and summed in bfloat16 or wider, within the bound.
A program may use at most 128 MiB of HBM per device.

v0:
```python
import jax
import jax.numpy as jnp
from jax import lax
from jax.sharding import PartitionSpec as P

TILE = 64


def spread(tile_flags):
    wide = jnp.repeat(jnp.repeat(tile_flags, TILE, 0), TILE, 1)
    return wide.astype(jnp.bfloat16)


def local(amplitudes, integrals, amp_mask, int_mask, pair_map):
    row_index = lax.axis_index("row")
    col_index = lax.axis_index("col")
    rows_here = amplitudes.shape[0]
    amp_cols = amplitudes.shape[1]
    row_tiles = rows_here // TILE
    amp_ktiles = amp_cols // TILE
    chosen = lax.dynamic_slice_in_dim(pair_map, row_index * row_tiles, row_tiles, 0)
    tile_rows = lax.dynamic_slice_in_dim(amp_mask, row_index * row_tiles, row_tiles, 0)
    tile_mask = lax.dynamic_slice_in_dim(tile_rows, col_index * amp_ktiles, amp_ktiles, 1)
    masked_amp = amplitudes * spread(tile_mask)
    int_rows = integrals.shape[0]
    out_cols = integrals.shape[1]
    int_ktiles = int_rows // TILE
    out_tiles = out_cols // TILE
    int_flags = lax.dynamic_slice(
        int_mask, (row_index * int_ktiles, col_index * out_tiles), (int_ktiles, out_tiles)
    )
    masked_int = integrals * spread(int_flags)
    full_amp = lax.all_gather(masked_amp, "col", axis=1, tiled=True)
    summed = jnp.dot(
        full_amp,
        lax.all_gather(masked_int, "row", axis=0, tiled=True),
        preferred_element_type=jnp.float32,
    )
    product = summed.astype(jnp.bfloat16)
    every_tile = lax.all_gather(product, "row", axis=0, tiled=True)
    return every_tile.reshape(-1, TILE, out_cols)[chosen].reshape(rows_here, out_cols)


def solution(mesh):
    in_specs = (P("row", "col"), P("row", "col"), P(), P(), P())
    out_specs = P("row", "col")
    return jax.shard_map(local, mesh=mesh, in_specs=in_specs, out_specs=out_specs, check_vma=False)
```

profile of v0, /device:TPU:1, one launch (start us, length us, event | category | flops | bytes accessed | tf_op | source)
XLA Modules:
  0.0 367.0 jit_solution(2655727340567959572)
XLA Ops:
  6.5 0.0 all-gather.6.cloned.1.call-start
  6.5 0.8 dynamic-slice_convert_fusion
  7.3 0.1 copy.8
  7.4 0.1 broadcast_in_dim.17
  7.5 0.1 convert_element_type.29
  7.6 2.9 copy.9
  10.5 0.0 copy-start
  10.5 1.5 bitcast_multiply_fusion
  12.0 0.0 all-gather.6.cloned.1.call-update
  12.0 0.0 all-gather.4.cloned.1.call-start
  12.1 0.8 dynamic-slice_convert_fusion.1
  12.8 0.1 broadcast_in_dim.15
  12.9 0.1 convert_element_type.26
  13.0 0.0 copy-done
  13.0 0.2 copy.7
  13.2 0.9 bitcast_multiply_fusion.1
  14.1 0.0 all-gather.4.cloned.1.call-update
  14.1 0.0 all-gather.8.cloned.1.call-start
  14.2 84.3 %all-gather.6.cloned.1.call-done = bf16[4096,1024]{0,1:T(8,128)(2,1)} async-done(((bf16[1024,1024]{0,1:T(8,128)(2,1)}), bf16[4096,1024]{0,1:T(8,128)(2,1)}) %all-gather.6.cloned.1.call-update) | async-done | bytes 8388624 | tf_op jit(solution)/shard_map/all_gather | solution.py:36
  98.5 76.3 %all-gather.4.cloned.1.call-done = bf16[2048,4096]{0,1:T(8,128)(2,1)} async-done(((bf16[2048,128]{0,1:T(8,128)(2,1)}), bf16[2048,4096]{0,1:T(8,128)(2,1)}) %all-gather.4.cloned.1.call-update) | async-done | bytes 16777232 | tf_op jit(solution)/shard_map/all_gather | solution.py:33
  174.8 23.9 %convolution_convert_fusion = bf16[2048,1024]{1,0:T(8,128)(2,1)} fusion(bf16[2048,4096]{0,1:T(8,128)(2,1)} %all-gather.4.cloned.1.call-done, bf16[4096,1024]{0,1:T(8,128)(2,1)} %all-gather.6.cloned.1.call-done), kind=kOutput, calls=%fused_computation.1 | convolution fusion | flops 17181966336 | bytes 29360128 | tf_op jit(solution)/shard_map/dot_general | solution.py:34
  198.6 0.0 copy-start.1
  198.6 0.0 all-gather.8.cloned.1.call-update
  198.7 0.6 copy-done.1
  199.3 0.1 compare_select_fusion
  199.4 152.5 %all-gather.8.cloned.1.call-done = bf16[8192,1024]{1,0:T(8,128)(2,1)} async-done(((bf16[2048,1024]{1,0:T(8,128)(2,1)}), bf16[8192,1024]{1,0:T(8,128)(2,1)}) %all-gather.8.cloned.1.call-update) | async-done | bytes 16777232 | tf_op jit(solution)/shard_map/all_gather | solution.py:40
  351.9 8.6 %gather_fusion = bf16[32,64,1024]{2,1,0:T(8,128)(2,1)} fusion(bf16[128,64,1024]{2,1,0:T(8,128)(2,1)} %bitcast.12, s32[1024]{0:T(1024)S(1)} %pad_clamp_fusion), kind=kCustom, calls=%fused_computation | custom fusion | bytes 8388736 | tf_op jit(solution)/shard_map/gather | solution.py:41
  (1 shorter events, 0.0 us)
Async XLA Ops:
  6.5 91.9 %all-gather.6.cloned.1.call-start = ((), (), s32[]{:S(2)}) async-start(), calls=%async_computation.1 | async-start | bytes 10485760 | tf_op jit(solution)/shard_map/all_gather | solution.py:36
  10.5 2.5 copy-start
  12.0 162.8 %all-gather.4.cloned.1.call-start = ((), (), s32[]{:S(2)}) async-start(), calls=%async_computation | async-start | bytes 17301504 | tf_op jit(solution)/shard_map/all_gather | solution.py:33
  14.1 337.8 %all-gather.8.cloned.1.call-start = ((), (), s32[]{:S(2)}) async-start(), calls=%async_computation.2 | async-start | bytes 20971520 | tf_op jit(solution)/shard_map/all_gather | solution.py:40
  198.6 0.7 copy-start.1
Sparse Core Ops, SparseCore 0:
  12.1 86.3 all-gather.5
  100.7 73.9 all-gather.3
  198.8 153.0 all-gather.7
where the time goes:
time: 367 us
  waiting for transfers between devices  313 us (85%)
  matrix products  23.9 us (7%)
  between operations  13.2 us (4%)
  local copies, waits for them, and re-layouts  12.8 us (3%)
  other arithmetic  3.97 us (1%)
    all_gather x1, waiting for transfers between devices, local(): every_tile = lax.all_gather(product, 'row', axis=0, tiled=True)  153 us
    all_gather x1, waiting for transfers between devices, local(): lax.all_gather(masked_int, 'row', axis=0, tiled=True)  84.3 us
    all_gather x1, waiting for transfers between devices, local(): full_amp = lax.all_gather(masked_amp, 'col', axis=1, tiled=True)  76.3 us
    dot_general x1, matrix products, local(): jnp.dot(full_amp, lax.all_gather(masked_int, 'row', axis=0, tiled=True),...  23.9 us
    gather x1, local copies, waits for them, and re-layouts, local(): every_tile.reshape(-1, TILE, out_cols)[chosen].reshape(rows_here, out_cols)  8.6 us
  transfers between devices with their start and end apart: 3, of which 3 were waited for; matrix products, arithmetic and copies ran while one was open for 1% of the time, Pallas kernels for 0%

commit v1 on v0

v1 whole, which is shorter than its diff:
```python
import jax
import jax.numpy as jnp
from jax import lax
from jax.sharding import PartitionSpec as P

TILE = 64


def spread(tile_flags):
    wide = jnp.repeat(jnp.repeat(tile_flags, TILE, 0), TILE, 1)
    return wide.astype(jnp.bfloat16)


def local(amplitudes, integrals, amp_mask, int_mask, pair_map):
    row_index = lax.axis_index("row")
    col_index = lax.axis_index("col")
    rows_here, amp_cols = amplitudes.shape
    row_tiles = rows_here // TILE
    amp_ktiles = amp_cols // TILE
    chosen = lax.dynamic_slice_in_dim(pair_map, row_index * row_tiles, row_tiles, 0)
    int_rows, out_cols = integrals.shape
    int_ktiles = int_rows // TILE
    out_tiles = out_cols // TILE
    int_flags = lax.dynamic_slice(
        int_mask, (row_index * int_ktiles, col_index * out_tiles), (int_ktiles, out_tiles)
    )
    masked_int = integrals * spread(int_flags)
    every_amp = lax.all_gather(amplitudes, "row", axis=0, tiled=True)
    picked = every_amp.reshape(-1, TILE, amp_cols)[chosen].reshape(rows_here, amp_cols)
    flag_cols = lax.dynamic_slice_in_dim(amp_mask, col_index * amp_ktiles, amp_ktiles, 1)
    masked_amp = picked * spread(flag_cols[chosen])
    full_amp = lax.all_gather(masked_amp, "col", axis=1, tiled=True)
    full_int = lax.all_gather(masked_int, "row", axis=0, tiled=True)
    summed = jnp.dot(full_amp, full_int, preferred_element_type=jnp.float32)
    return summed.astype(jnp.bfloat16)


def solution(mesh):
    in_specs = (P("row", "col"), P("row", "col"), P(), P(), P())
    out_specs = P("row", "col")
    return jax.shard_map(local, mesh=mesh, in_specs=in_specs, out_specs=out_specs, check_vma=False)
```

time: 367 us -> 243 us (0.66)
  waiting for transfers between devices: 313 us -> 196 us
  local copies, waits for them, and re-layouts: 12.8 us -> 6.7 us
    all_gather x2, waiting for transfers between devices: 237 us -> 110 us  [the longest x1 81.6 us: local(): full_int = lax.all_gather(masked_int, 'row', axis=0, tiled=True)]
    all_gather x1, waiting for transfers between devices: 76.3 us -> 84.8 us  [local(): full_amp = lax.all_gather(masked_amp, 'col', axis=1, tiled=True)]
    gather x1 -> x3, local copies, waits for them, and re-layouts: 8.6 us -> 2.89 us  [the longest x1 2.24 us: local(): every_amp.reshape(-1, TILE, amp_cols)[chosen].reshape(rows_here, amp_cols)]
  transfers between devices with their start and end apart: 3 -> 3, of which waited for: 3 -> 3; matrix products, arithmetic and copies ran while one was open for 1% -> 4% of each run, Pallas kernels for 0% -> 0%
where the time goes in v1:
time: 243 us
  waiting for transfers between devices  196 us (81%)
  matrix products  23.8 us (10%)
  between operations  13.2 us (5%)
  local copies, waits for them, and re-layouts  6.7 us (3%)
  other arithmetic  3.29 us (1%)
    all_gather x1, waiting for transfers between devices, local(): full_amp = lax.all_gather(masked_amp, 'col', axis=1, tiled=True)  84.8 us
    all_gather x1, waiting for transfers between devices, local(): full_int = lax.all_gather(masked_int, 'row', axis=0, tiled=True)  81.6 us
    all_gather x1, waiting for transfers between devices, local(): every_amp = lax.all_gather(amplitudes, 'row', axis=0, tiled=True)  28.9 us
    dot_general x1, matrix products, local(): summed = jnp.dot(full_amp, full_int, preferred_element_type=jnp.float32)  23.8 us
  transfers between devices with their start and end apart: 3, of which 3 were waited for; matrix products, arithmetic and copies ran while one was open for 4% of the time, Pallas kernels for 0%

profile of v1, /device:TPU:1, one launch (start us, length us, event | category | flops | bytes accessed | tf_op | source)
XLA Modules:
  0.0 243.0 jit_solution(8455773712610641382)
XLA Ops:
  6.5 0.0 copy-start
  6.5 0.0 all-gather.4.cloned.1.call-start
  6.5 0.7 all-gather.4.cloned.1.call-update
  7.3 0.0 all-gather.8.cloned.1.call-start
  7.3 0.8 dynamic-slice_convert_fusion
  8.1 0.1 copy.19
  8.2 0.1 broadcast_in_dim.19
  8.3 0.1 convert_element_type.29
  8.4 2.9 %copy.20 = bf16[1024,1024]{0,1:T(8,128)(2,1)S(1)} copy(bf16[1024,1024]{1,0:T(8,128)(2,1)} %param.6) | data formatting | bytes 4194304 | tf_op args[1]
  11.3 0.0 copy-start.1
  11.3 1.5 bitcast_multiply_fusion
  12.8 0.0 all-gather.8.cloned.1.call-update
  12.8 0.0 all-gather.6.cloned.1.call-start
  12.8 0.0 copy-done
  12.9 0.1 copy.21
  13.0 0.0 copy-done.1
  13.0 0.1 compare_select_fusion
  13.1 0.6 gather_fusion.1
  13.6 0.1 copy.17
  13.7 0.1 broadcast_in_dim.17
  13.8 0.1 convert_element_type.26
  13.9 0.1 broadcast_in_dim.18
  14.0 0.3 copy.18
  14.3 28.9 %all-gather.4.cloned.1.call-done = bf16[8192,128]{1,0:T(8,128)(2,1)} async-done(((bf16[2048,128]{1,0:T(8,128)(2,1)}), bf16[8192,128]{1,0:T(8,128)(2,1)}) %all-gather.4.cloned.1.call-update) | async-done | bytes 2097168 | tf_op jit(solution)/shard_map/all_gather | solution.py:28
  43.1 2.2 gather_fusion
  45.4 0.9 bitcast_multiply_fusion.1
  46.3 0.0 all-gather.6.cloned.1.call-update
  46.3 81.6 %all-gather.8.cloned.1.call-done = bf16[4096,1024]{0,1:T(8,128)(2,1)} async-done(((bf16[1024,1024]{0,1:T(8,128)(2,1)}), bf16[4096,1024]{0,1:T(8,128)(2,1)}) %all-gather.8.cloned.1.call-update) | async-done | bytes 8388624 | tf_op jit(solution)/shard_map/all_gather | solution.py:33
  127.9 84.8 %all-gather.6.cloned.1.call-done = bf16[2048,4096]{1,0:T(8,128)(2,1)} async-done(((bf16[2048,128]{1,0:T(8,128)(2,1)}), bf16[2048,4096]{1,0:T(8,128)(2,1)}) %all-gather.6.cloned.1.call-update) | async-done | bytes 16777232 | tf_op jit(solution)/shard_map/all_gather | solution.py:32
  212.8 23.8 %convolution_convert_fusion = bf16[2048,1024]{1,0:T(8,128)(2,1)} fusion(bf16[2048,4096]{1,0:T(8,128)(2,1)} %all-gather.6.cloned.1.call-done, bf16[4096,1024]{0,1:T(8,128)(2,1)} %all-gather.8.cloned.1.call-done), kind=kOutput, calls=%fused_computation.2 | convolution fusion | flops 17181966336 | bytes 29360128 | tf_op jit(solution)/shard_map/dot_general | solution.py:34
  (3 shorter events, 0.0 us)
Async XLA Ops:
  6.5 6.3 %copy-start = (s32[128,64]{0,1:T(8,128)S(1)}, s32[128,64]{0,1:T(8,128)}, u32[]{:S(2)}) copy-start(s32[128,64]{0,1:T(8,128)} %param.7) | copy-start | bytes 98308
  6.5 36.6 %all-gather.4.cloned.1.call-start = ((), (), s32[]{:S(2)}) async-start(), calls=%async_computation | async-start | bytes 2621440 | tf_op jit(solution)/shard_map/all_gather | solution.py:28
  7.3 120.7 %all-gather.8.cloned.1.call-start = ((), (), s32[]{:S(2)}) async-start(), calls=%async_computation.2 | async-start | bytes 10485760 | tf_op jit(solution)/shard_map/all_gather | solution.py:33
  11.3 1.7 copy-start.1
  12.8 200.0 %all-gather.6.cloned.1.call-start = ((), (), s32[]{:S(2)}) async-start(), calls=%async_computation.1 | async-start | bytes 17301504 | tf_op jit(solution)/shard_map/all_gather | solution.py:32
Sparse Core Ops, SparseCore 0:
  9.0 34.0 all-gather.3
  44.8 83.1 all-gather.7
  130.1 82.5 all-gather.5

commit v2 on v1

v2 whole, which is shorter than its diff:
```python
import jax
import jax.numpy as jnp
from jax import lax
from jax.experimental import pallas as pl
from jax.experimental.pallas import tpu as pltpu
from jax.sharding import PartitionSpec as P

TILE = 64
MESH = pl.DeviceIdType.MESH
CHUNKS = 4
WIDE = 256
ROWS_STEP = 512


class Ring:
    def __init__(self, slot, down, up, send, recv, own=None):
        own = own or (lambda half: slot(0, half))
        routes = (
            (own(0), slot(0, 0), up),
            (own(1), slot(0, 1), down),
            (own(1), slot(0, 1), up),
            (own(0), slot(0, 0), down),
            (slot(-1, 0), slot(-1, 0), up),
            (slot(1, 1), slot(1, 1), down),
        )
        self.copies = [
            pltpu.make_async_remote_copy(
                src_ref=src, dst_ref=dst, send_sem=send.at[i], recv_sem=recv.at[i], device_id=to, device_id_type=MESH
            )
            for i, (src, dst, to) in enumerate(routes)
        ]

    def start(self):
        for copy in self.copies[:4]:
            copy.start()

    def forward(self):
        for i in (0, 1):
            self.copies[i].wait_recv()
            self.copies[4 + i].start()

    def near(self):
        for copy in self.copies[2:4]:
            copy.wait_recv()

    def far(self):
        for copy in self.copies[4:]:
            copy.wait_recv()

    def finish(self):
        for copy in self.copies:
            copy.wait_send()


def kernel(
    amp_mask, pair_map, int_mask, amp, ints, out,
    amp_all, full, ints_in, flag_rows, ints_all, stage, total,
    ring_send, ring_recv, relay_send, relay_recv, local_sem, out_sem,
):
    y = lax.axis_index("row")
    col = lax.axis_index("col")
    core = lax.rem(col, 2)
    x = lax.rem(lax.div(col, 2), 4)
    z = lax.div(col, 8)

    def turn(a, d):
        return lax.rem(a + (d + 4), 4)

    def place(dx, dz, c):
        return turn(z, dz) * 8 + turn(x, dx) * 2 + c

    up_y, down_y = (turn(y, 1), col), (turn(y, -1), col)
    up_x, down_x = (y, place(1, 0, core)), (y, place(-1, 0, core))
    up_z, down_z = (y, place(0, 1, core)), (y, place(0, -1, core))
    twin = (y, place(0, 0, 1 - core))

    amp_in = pltpu.make_async_copy(amp, amp_all.at[pl.ds(y * 32, 32)], local_sem.at[0])
    ints_copy = pltpu.make_async_copy(ints, ints_in, local_sem.at[1])
    ints_copy.start()
    amp_in.start()

    barrier = pltpu.get_barrier_semaphore()
    for other in (up_y, down_y, up_x, down_x, up_z, down_z, twin):
        pl.semaphore_signal(barrier, inc=1, device_id=other, device_id_type=MESH)
    pl.semaphore_wait(barrier, 7)

    used = [0]

    def ring(slot, down, up, own=None):
        n = used[0]
        used[0] += 1
        return Ring(slot, down, up, ring_send.at[n], ring_recv.at[n], own)

    ring_a = ring(
        lambda d, half: amp_all.at[pl.ds(turn(y, d) * 32 + half * 16, 16)],
        down_y, up_y, lambda half: amp.at[pl.ds(half * 16, 16)],
    )
    ring_a.start()

    wide = CHUNKS * WIDE
    chosen = lax.broadcasted_iota(jnp.int32, (512, wide), 0)
    lane_tile = lax.broadcasted_iota(jnp.int32, (512, wide), 1) >> 6
    pick = jnp.where(chosen == lane_tile + col * 16, 1.0, 0.0).astype(jnp.bfloat16)
    flags = int_mask[pl.ds(pl.multiple_of(y * 16, 16), 16), :].astype(jnp.float32).astype(jnp.bfloat16)
    flag_rows[...] = jnp.dot(flags, pick, preferred_element_type=jnp.float32)
    ints_copy.wait()
    for j in range(CHUNKS):
        for t in range(16):
            flag = flag_rows[t : t + 1, j * WIDE : (j + 1) * WIDE]
            spread = jnp.broadcast_to(flag, (TILE, WIDE)).astype(jnp.bfloat16)
            block = ints_in[t * TILE : (t + 1) * TILE, j * WIDE : (j + 1) * WIDE]
            ints_all[j, pl.ds(pl.multiple_of(y * 1024 + t * TILE, TILE), TILE), :] = block * spread

    def ring_of_chunk(j):
        return ring(
            lambda d, half: ints_all.at[j, pl.ds(pl.multiple_of(turn(y, d) * 1024 + half * 512, 512), 512)],
            down_y, up_y,
        )

    ring_b = [ring_of_chunk(j) for j in range(CHUNKS)]

    ring_a.forward()
    ring_a.near()
    ring_b[0].start()
    amp_in.wait()
    ring_a.far()

    lane = lax.broadcasted_iota(jnp.int32, (TILE, 128), 1)

    def choose(q, carry):
        tile = pair_map[y * 32 + q]
        left = amp_mask[tile, col * 2]
        right = amp_mask[tile, col * 2 + 1]
        flag = jnp.where(lane < TILE, left, right).astype(jnp.float32).astype(jnp.bfloat16)
        full[col, pl.ds(pl.multiple_of(q * TILE, TILE), TILE), :] = amp_all[tile] * flag
        return carry

    lax.fori_loop(0, 32, choose, 0)

    relays = []

    def relay(dx, dz, start, size):
        n = len(relays)
        piece = full.at[place(dx, dz, core), pl.ds(start, size)]
        copy = pltpu.make_async_remote_copy(
            src_ref=piece, dst_ref=piece, send_sem=relay_send.at[n], recv_sem=relay_recv.at[n],
            device_id=twin, device_id_type=MESH,
        )
        copy.start()
        relays.append(copy)

    def rows_of(part, half):
        return pl.ds(part * 1024 + half * 512, 512)

    def ring_x(part, dz):
        return ring(lambda d, half: full.at[place(d, dz, core), rows_of(part, half)], down_x, up_x)

    def ring_z(part, dx):
        return ring(lambda d, half: full.at[place(dx, d, core), rows_of(part, half)], down_z, up_z)

    first_x, first_z = ring_x(0, 0), ring_z(1, 0)
    then_z = {d: ring_z(0, d) for d in (0, -1, 1, 2)}
    then_x = {d: ring_x(1, d) for d in (0, -1, 1, 2)}
    first_x.start()
    first_z.start()
    relay(0, 0, 0, 2048)
    then_z[0].start()
    then_x[0].start()
    first_x.forward()
    first_z.forward()
    ring_b[0].forward()
    ring_b[1].start()
    first_x.near()
    first_z.near()
    for d in (-1, 1):
        then_z[d].start()
        then_x[d].start()
        relay(d, 0, 0, 1024)
        relay(0, d, 1024, 1024)
    first_x.far()
    first_z.far()
    then_z[2].start()
    then_x[2].start()
    relay(2, 0, 0, 1024)
    relay(0, 2, 1024, 1024)
    for d in (0, -1, 1, 2):
        then_z[d].forward()
        then_x[d].forward()
        then_z[d].near()
        then_x[d].near()
        for e in (-1, 1):
            relay(d, e, 0, 1024)
            relay(e, d, 1024, 1024)
        if d == -1:
            ring_b[1].forward()
            ring_b[2].start()
    for d in (0, -1, 1, 2):
        then_z[d].far()
        then_x[d].far()
        relay(d, 2, 0, 1024)
        relay(2, d, 1024, 1024)
    ring_b[2].forward()
    ring_b[3].start()
    for copy in relays:
        copy.wait_recv()

    def result(j):
        return pltpu.make_async_copy(
            stage.at[j % 2], out.at[:, pl.ds(j * WIDE, WIDE)], out_sem.at[j]
        )

    def lines(m):
        return pl.ds(pl.multiple_of(m * ROWS_STEP, ROWS_STEP), ROWS_STEP)

    def whole(j):
        def step(m, carry):
            left = jnp.concatenate([full[s, lines(m), :] for s in range(32)], axis=1)
            stage[j % 2, lines(m), :] = jnp.dot(
                left, ints_all[j], preferred_element_type=jnp.float32
            ).astype(jnp.bfloat16)
            return carry

        lax.fori_loop(0, 2048 // ROWS_STEP, step, 0)
        result(j).start()

    def part(j, d, m):
        plane = turn(y, d)
        left = jnp.concatenate([full[plane * 8 + s, lines(m), :] for s in range(8)], axis=1)
        right = ints_all[j, pl.ds(pl.multiple_of(plane * 1024, 1024), 1024), :]
        return jnp.dot(left, right, preferred_element_type=jnp.float32)

    def over_rows(body):
        def step(m, carry):
            body(m)
            return carry

        lax.fori_loop(0, 2048 // ROWS_STEP, step, 0)

    ring_b[0].near()
    ring_b[0].far()
    whole(0)
    ring_b[1].near()
    ring_b[1].far()
    whole(1)
    ring_b[3].forward()
    ring_b[2].near()
    ring_b[2].far()
    result(0).wait()
    whole(2)

    last = CHUNKS - 1

    def begin(m):
        total[lines(m), :] = part(last, 0, m)

    def add(d):
        def body(m):
            total[lines(m), :] += part(last, d, m)

        return body

    def end(m):
        stage[last % 2, lines(m), :] = (total[lines(m), :] + part(last, 2, m)).astype(jnp.bfloat16)

    over_rows(begin)
    ring_b[3].near()
    over_rows(add(-1))
    over_rows(add(1))
    result(1).wait()
    ring_b[3].far()
    over_rows(end)
    result(last).start()

    for each in (ring_a, *ring_b, first_x, first_z, *then_z.values(), *then_x.values()):
        each.finish()
    for copy in relays:
        copy.wait_send()
    result(2).wait()
    result(last).wait()


def local(amplitudes, integrals, amp_mask, int_mask, pair_map):
    rings = 15
    relays = 31
    anywhere = pl.BlockSpec(memory_space=pl.ANY)
    return pl.pallas_call(
        kernel,
        out_shape=jax.ShapeDtypeStruct((2048, 1024), jnp.bfloat16),
        in_specs=[
            pl.BlockSpec(memory_space=pltpu.SMEM),
            pl.BlockSpec(memory_space=pltpu.SMEM),
            pl.BlockSpec(memory_space=pltpu.VMEM),
            anywhere,
            anywhere,
        ],
        out_specs=anywhere,
        scratch_shapes=[
            pltpu.VMEM((128, TILE, 128), jnp.bfloat16),
            pltpu.VMEM((32, 2048, 128), jnp.bfloat16),
            pltpu.VMEM((1024, 1024), jnp.bfloat16),
            pltpu.VMEM((16, 1024), jnp.float32),
            pltpu.VMEM((CHUNKS, 4096, WIDE), jnp.bfloat16),
            pltpu.VMEM((2, 2048, WIDE), jnp.bfloat16),
            pltpu.VMEM((2048, WIDE), jnp.float32),
            pltpu.SemaphoreType.DMA((rings, 6)),
            pltpu.SemaphoreType.DMA((rings, 6)),
            pltpu.SemaphoreType.DMA((relays,)),
            pltpu.SemaphoreType.DMA((relays,)),
            pltpu.SemaphoreType.DMA((2,)),
            pltpu.SemaphoreType.DMA((CHUNKS,)),
        ],
        compiler_params=pltpu.CompilerParams(
            collective_id=0, has_side_effects=True, vmem_limit_bytes=56 * 1024 * 1024
        ),
        cost_estimate=pl.CostEstimate(flops=2 * 2048 * 4096 * 1024, bytes_accessed=7 * 2**20, transcendentals=0),
    )(amp_mask, pair_map, int_mask, amplitudes.reshape(32, TILE, 128), integrals)


def solution(mesh):
    in_specs = (P("row", "col"), P("row", "col"), P(), P(), P())
    out_specs = P("row", "col")
    return jax.shard_map(local, mesh=mesh, in_specs=in_specs, out_specs=out_specs, check_vma=False)
```

time: 243 us -> 107 us (0.44)
  waiting for transfers between devices: 196 us -> 0 us
  Pallas kernels: 0 us -> 99.7 us
  matrix products: 23.8 us -> 0 us
  between operations: 13.2 us -> 0.01 us
  other arithmetic: 3.29 us -> 0 us
    all_gather x3 -> x0, waiting for transfers between devices: 195 us -> none  [the longest x1 84.8 us: local(): full_amp = lax.all_gather(masked_amp, 'col', axis=1, tiled=True)]
    pallas_call x0 -> x1, Pallas kernels: none -> 99.7 us  [local(): pl.pallas_call(kernel, out_shape=jax.ShapeDtypeStruct((2048, 1024), jnp.b...]
    dot_general x1 -> x0, matrix products: 23.8 us -> none  [local(): summed = jnp.dot(full_amp, full_int, preferred_element_type=jnp.float32)]
    unnamed x6 -> x2, local copies, waits for them, and re-layouts: 2.99 us -> 6.13 us
    gather x3 -> x0, local copies, waits for them, and re-layouts: 2.89 us -> none  [the longest x1 2.24 us: local(): every_amp.reshape(-1, TILE, amp_cols)[chosen].reshape(rows_here, amp_cols)]
  transfers between devices with their start and end apart: 3 -> 0, of which waited for: 3 -> 0; matrix products, arithmetic and copies ran while one was open for 4% -> 0% of each run, Pallas kernels for 0% -> 0%
where the time goes in v2:
time: 107 us; the launch traced here: 106 us
  Pallas kernels  99.7 us (93%)
  local copies, waits for them, and re-layouts  6.13 us (6%)
    pallas_call x1, Pallas kernels, local(): pl.pallas_call(kernel, out_shape=jax.ShapeDtypeStruct((2048, 1024), jnp.b...  99.7 us
    unnamed x2, local copies, waits for them, and re-layouts  6.13 us

profile of v2, /device:TPU:1, one launch (start us, length us, event | category | flops | bytes accessed | tf_op | source)
XLA Modules:
  0.0 105.8 jit_solution(695152156175417644)
XLA Ops:
  0.0 1.5 %copy.6.amp_mask = s32[128,64]{1,0:T(8,128)} copy(s32[128,64]{0,1:T(8,128)} %param.7) | data formatting | bytes 65536 | tf_op args[2]
  1.5 99.7 %shard_map.55 = bf16[2048,1024]{1,0:T(8,128)(2,1)} custom-call(s32[128,64]{1,0:T(8,128)} %copy.6.amp_mask, s32[128]{0:T(128)} %pair_map.1, s32[64,512]{1,0:T(8,128)} %int_mask.1, bf16[32,64,128]{2,1,0:T(8,128)(2,1)} %bitcast.1, bf16[1024,1024]{1,0:T(8,128)(2,1)} %ints.1), custom_call_target="tpu_custom_call" | custom-call | flops 17179869184 | bytes 7340032 | tf_op jit(solution)/shard_map/pallas_call | solution.py:286
  101.2 4.6 %copy.8 = bf16[2048,1024]{1,0:T(8,128)(2,1)} copy(bf16[2048,1024]{1,0:T(8,128)(2,1)} %shard_map.55) | data formatting | bytes 8388608

commit v3 on v2

v3 whole, which is shorter than its diff:
```python
import jax
import jax.numpy as jnp
from jax import lax
from jax.experimental import pallas as pl
from jax.experimental.pallas import tpu as pltpu
from jax.sharding import PartitionSpec as P

TILE = 64
HALF = TILE // 2
MESH = pl.DeviceIdType.MESH
CHUNKS = 4
WIDE = 256
ROWS_STEP = 512
RINGS = CHUNKS + 10
RELAYS = 31


class Ring:
    def __init__(self, slot, down, up, send, recv):
        routes = (
            (slot(0, 0), up),
            (slot(0, 1), down),
            (slot(0, 1), up),
            (slot(0, 0), down),
            (slot(-1, 0), up),
            (slot(1, 1), down),
        )
        self.copies = [
            pltpu.make_async_remote_copy(
                src_ref=piece, dst_ref=piece, send_sem=send.at[i], recv_sem=recv.at[i], device_id=to, device_id_type=MESH
            )
            for i, (piece, to) in enumerate(routes)
        ]

    def start_first(self):
        for copy in self.copies[:2]:
            copy.start()

    def start_second(self):
        for copy in self.copies[2:4]:
            copy.start()

    def start(self):
        self.start_first()
        self.start_second()

    def forward(self):
        for i in (0, 1):
            self.copies[i].wait_recv()
            self.copies[4 + i].start()

    def near(self):
        for copy in self.copies[2:4]:
            copy.wait_recv()

    def far(self):
        for copy in self.copies[4:]:
            copy.wait_recv()

    def finish(self):
        for copy in self.copies:
            copy.wait_send()


def kernel(
    amp_mask_in, pair_map_in, int_mask_in, amp, ints, out,
    amp_mask, pair_map, int_mask, known_0, known_1, packed_0, packed_1, got_0, got_1,
    full, ints_in, flag_rows, ints_all, total,
    ring_send, ring_recv, swap_send, swap_recv, relay_send, relay_recv, local_sem,
):
    y = lax.axis_index("row")
    col = lax.axis_index("col")
    core = lax.rem(col, 2)
    x = lax.rem(lax.div(col, 2), 4)
    z = lax.div(col, 8)

    def turn(a, d):
        return lax.rem(a + (d + 4), 4)

    def place(dx, dz, c):
        return turn(z, dz) * 8 + turn(x, dx) * 2 + c

    up_y, down_y = (turn(y, 1), col), (turn(y, -1), col)
    up_x, down_x = (y, place(1, 0, core)), (y, place(-1, 0, core))
    up_z, down_z = (y, place(0, 1, core)), (y, place(0, -1, core))
    twin = (y, place(0, 0, 1 - core))

    barrier = pltpu.get_barrier_semaphore()
    for other in (up_y, down_y, up_x, down_x, up_z, down_z, twin):
        pl.semaphore_signal(barrier, inc=1, device_id=other, device_id_type=MESH)

    known, packed, got = (known_0, known_1), (packed_0, packed_1), (got_0, got_1)

    def half_rows(h):
        return amp.at[:, pl.ds(h * HALF, HALF)]

    mask_row = pl.multiple_of(lax.div(col, 4) * 8, 8)
    own_row = pl.multiple_of(y * 16, 16)
    ints_copy = pltpu.make_async_copy(ints, ints_in, local_sem.at[0])
    int_mask_copy = pltpu.make_async_copy(int_mask_in.at[pl.ds(own_row, 16)], int_mask, local_sem.at[1])
    amp_copies = [
        pltpu.make_async_copy(amp_mask_in.at[pl.ds(mask_row, 8)], amp_mask, local_sem.at[2]),
        pltpu.make_async_copy(pair_map_in, pair_map, local_sem.at[3]),
        pltpu.make_async_copy(half_rows(0), known_0.at[pl.ds(0, 32)], local_sem.at[4]),
        pltpu.make_async_copy(half_rows(1), known_1.at[pl.ds(0, 32)], local_sem.at[5]),
    ]
    for copy in (int_mask_copy, ints_copy, *amp_copies):
        copy.start()

    odd = lax.rem(y, 2)
    even_odd = y + 1 - 2 * odd
    odd_even = lax.rem(y + 3 + 2 * odd, 4)
    first, second = (even_odd, odd_even), (odd_even, even_odd)

    def swap(n, src, dst, to):
        return pltpu.make_async_remote_copy(
            src_ref=src, dst_ref=dst, send_sem=swap_send.at[n], recv_sem=swap_recv.at[n],
            device_id=(to, col), device_id_type=MESH,
        )

    swap_all = [swap(h, half_rows(h), known[h].at[pl.ds(32, 32)], first[h]) for h in (0, 1)]
    swap_some = [swap(2 + h, packed[h], got[h], second[h]) for h in (0, 1)]

    pl.semaphore_wait(barrier, 7)
    for copy in swap_all:
        copy.start()

    wide = CHUNKS * WIDE
    chosen = lax.broadcasted_iota(jnp.int32, (512, wide), 0)
    lane_tile = lax.broadcasted_iota(jnp.int32, (512, wide), 1) >> 6
    pick = jnp.where(chosen == lane_tile + col * 16, 1.0, 0.0).astype(jnp.bfloat16)
    int_mask_copy.wait()
    flags = int_mask[...].astype(jnp.float32).astype(jnp.bfloat16)
    flag_rows[...] = jnp.dot(flags, pick, preferred_element_type=jnp.float32)
    ints_copy.wait()

    def mask_chunk(j):
        for t in range(16):
            flag = flag_rows[t : t + 1, j * WIDE : (j + 1) * WIDE]
            spread = jnp.broadcast_to(flag, (TILE, WIDE)).astype(jnp.bfloat16)
            block = ints_in[t * TILE : (t + 1) * TILE, j * WIDE : (j + 1) * WIDE]
            ints_all[j, pl.ds(pl.multiple_of(y * 1024 + t * TILE, TILE), TILE), :] = block * spread

    used = [0]

    def ring(slot, down, up):
        n = used[0]
        used[0] += 1
        return Ring(slot, down, up, ring_send.at[n], ring_recv.at[n])

    def ring_of_chunk(j):
        return ring(
            lambda d, half: ints_all.at[j, pl.ds(pl.multiple_of(turn(y, d) * 1024 + half * 512, 512), 512)],
            down_y, up_y,
        )

    ring_b = [ring_of_chunk(j) for j in range(CHUNKS)]

    mask_chunk(0)
    ring_b[0].start_first()

    for copy in amp_copies:
        copy.wait()
    for h in (0, 1):
        swap_all[h].wait_recv()

        def pack(q, carry, h=h):
            tile = pair_map[second[h] * 32 + q]
            plane, at = tile >> 5, tile & 31
            here = jnp.where(plane == y, at, jnp.where(plane == first[h], at + 32, 0))
            packed[h][q] = known[h][here]
            return carry

        lax.fori_loop(0, 32, pack, 0)
        swap_some[h].start()
    ring_b[0].start_second()
    for j in range(1, CHUNKS):
        mask_chunk(j)
    for copy in swap_some:
        copy.wait_recv()

    lane = lax.broadcasted_iota(jnp.int32, (HALF, 128), 1)

    def choose(q, carry):
        tile = pair_map[y * 32 + q]
        plane, at = tile >> 5, tile & 31
        left = amp_mask[lax.rem(col, 4) * 2, tile]
        right = amp_mask[lax.rem(col, 4) * 2 + 1, tile]
        for h in (0, 1):
            mine = jnp.where(plane == y, 1, 0)
            theirs = jnp.where(plane == first[h], 1, 0)
            here = mine + theirs
            there = 1 - here

            def flag(side):
                return jnp.where(lane < TILE, left * side, right * side).astype(jnp.float32).astype(jnp.bfloat16)

            full[col, pl.ds(pl.multiple_of(q * TILE + h * HALF, HALF), HALF), :] = (
                known[h][at + 32 * theirs] * flag(here) + got[h][q] * flag(there)
            )
        return carry

    lax.fori_loop(0, 32, choose, 0)

    relays = []

    def relay(dx, dz, start, size):
        n = len(relays)
        piece = full.at[place(dx, dz, core), pl.ds(start, size)]
        copy = pltpu.make_async_remote_copy(
            src_ref=piece, dst_ref=piece, send_sem=relay_send.at[n], recv_sem=relay_recv.at[n],
            device_id=twin, device_id_type=MESH,
        )
        copy.start()
        relays.append(copy)

    def rows_of(part, half):
        return pl.ds(part * 1024 + half * 512, 512)

    def ring_x(part, dz):
        return ring(lambda d, half: full.at[place(d, dz, core), rows_of(part, half)], down_x, up_x)

    def ring_z(part, dx):
        return ring(lambda d, half: full.at[place(dx, d, core), rows_of(part, half)], down_z, up_z)

    first_x, first_z = ring_x(0, 0), ring_z(1, 0)
    then_z = {d: ring_z(0, d) for d in (0, -1, 1, 2)}
    then_x = {d: ring_x(1, d) for d in (0, -1, 1, 2)}
    first_x.start()
    first_z.start()
    relay(0, 0, 0, 2048)
    then_z[0].start()
    then_x[0].start()
    first_x.forward()
    first_z.forward()
    ring_b[0].forward()
    ring_b[1].start()
    first_x.near()
    first_z.near()
    for d in (-1, 1):
        then_z[d].start()
        then_x[d].start()
        relay(d, 0, 0, 1024)
        relay(0, d, 1024, 1024)
    first_x.far()
    first_z.far()
    then_z[2].start()
    then_x[2].start()
    relay(2, 0, 0, 1024)
    relay(0, 2, 1024, 1024)
    for d in (0, -1, 1, 2):
        then_z[d].forward()
        then_x[d].forward()
        then_z[d].near()
        then_x[d].near()
        for e in (-1, 1):
            relay(d, e, 0, 1024)
            relay(e, d, 1024, 1024)
        if d == -1:
            ring_b[1].forward()
            ring_b[2].start()
    for d in (0, -1, 1, 2):
        then_z[d].far()
        then_x[d].far()
        relay(d, 2, 0, 1024)
        relay(2, d, 1024, 1024)
    ring_b[2].forward()
    ring_b[3].start()
    for copy in relays:
        copy.wait_recv()

    def lines(m):
        return pl.ds(pl.multiple_of(m * ROWS_STEP, ROWS_STEP), ROWS_STEP)

    def over_rows(body):
        def step(m, carry):
            body(lines(m))
            return carry

        lax.fori_loop(0, 2048 // ROWS_STEP, step, 0)

    def whole(j):
        def body(rows):
            left = jnp.concatenate([full[s, rows, :] for s in range(32)], axis=1)
            out[rows, j * WIDE : (j + 1) * WIDE] = jnp.dot(
                left, ints_all[j], preferred_element_type=jnp.float32
            ).astype(jnp.bfloat16)

        over_rows(body)

    last = CHUNKS - 1

    def part(d, rows):
        plane = turn(y, d)
        left = jnp.concatenate([full[plane * 8 + s, rows, :] for s in range(8)], axis=1)
        right = ints_all[last, pl.ds(pl.multiple_of(plane * 1024, 1024), 1024), :]
        return jnp.dot(left, right, preferred_element_type=jnp.float32)

    def begin(rows):
        total[rows, :] = part(0, rows)

    def add(rows):
        total[rows, :] += part(-1, rows) + part(1, rows)

    def end(rows):
        out[rows, last * WIDE : (last + 1) * WIDE] = (total[rows, :] + part(2, rows)).astype(jnp.bfloat16)

    ring_b[0].near()
    ring_b[0].far()
    whole(0)
    ring_b[1].near()
    ring_b[1].far()
    whole(1)
    ring_b[3].forward()
    ring_b[2].near()
    ring_b[2].far()
    whole(2)
    over_rows(begin)
    ring_b[3].near()
    over_rows(add)
    ring_b[3].far()
    over_rows(end)

    for each in (*ring_b, first_x, first_z, *then_z.values(), *then_x.values()):
        each.finish()
    for copy in (*swap_all, *swap_some, *relays):
        copy.wait_send()


def local(amplitudes, integrals, amp_mask, int_mask, pair_map):
    anywhere = pl.BlockSpec(memory_space=pl.ANY)
    half_tiles = [pltpu.VMEM((n, HALF, 128), jnp.bfloat16) for n in (64, 64, 32, 32, 32, 32)]
    return pl.pallas_call(
        kernel,
        out_shape=pltpu.VMEM((2048, 1024), jnp.bfloat16),
        in_specs=[anywhere] * 5,
        out_specs=pl.BlockSpec(memory_space=pltpu.VMEM),
        scratch_shapes=[
            pltpu.SMEM((8, 128), jnp.int32),
            pltpu.SMEM((128,), jnp.int32),
            pltpu.VMEM((16, 512), jnp.int32),
            *half_tiles,
            pltpu.VMEM((32, 2048, 128), jnp.bfloat16),
            pltpu.VMEM((1024, 1024), jnp.bfloat16),
            pltpu.VMEM((16, 1024), jnp.float32),
            pltpu.VMEM((CHUNKS, 4096, WIDE), jnp.bfloat16),
            pltpu.VMEM((2048, WIDE), jnp.float32),
            pltpu.SemaphoreType.DMA((RINGS, 6)),
            pltpu.SemaphoreType.DMA((RINGS, 6)),
            pltpu.SemaphoreType.DMA((4,)),
            pltpu.SemaphoreType.DMA((4,)),
            pltpu.SemaphoreType.DMA((RELAYS,)),
            pltpu.SemaphoreType.DMA((RELAYS,)),
            pltpu.SemaphoreType.DMA((6,)),
        ],
        compiler_params=pltpu.CompilerParams(
            collective_id=0, has_side_effects=True, vmem_limit_bytes=52 * 1024 * 1024
        ),
        cost_estimate=pl.CostEstimate(flops=2 * 2048 * 4096 * 1024, bytes_accessed=7 * 2**20, transcendentals=0),
    )(amp_mask.T, pair_map, int_mask, amplitudes.reshape(32, TILE, 128), integrals)


def solution(mesh):
    in_specs = (P("row", "col"), P("row", "col"), P(), P(), P())
    out_specs = P("row", "col")
    return jax.shard_map(local, mesh=mesh, in_specs=in_specs, out_specs=out_specs, check_vma=False)
```

time: 107 us -> 98.8 us (0.923); the launches traced: 106 us -> 98.8 us
  local copies, waits for them, and re-layouts: 6.13 us -> 2.02 us
  Pallas kernels: 99.7 us -> 96.7 us
    unnamed x2 -> x1, local copies, waits for them, and re-layouts: 6.13 us -> 2.02 us
    pallas_call x1, Pallas kernels: 99.7 us -> 96.7 us  [local(): pl.pallas_call(kernel, out_shape=pltpu.VMEM((2048, 1024), jnp.bfloat16),...]
where the time goes in v3:
time: 98.8 us
  Pallas kernels  96.7 us (98%)
  local copies, waits for them, and re-layouts  2.02 us (2%)
    pallas_call x1, Pallas kernels, local(): pl.pallas_call(kernel, out_shape=pltpu.VMEM((2048, 1024), jnp.bfloat16),...  96.7 us
    unnamed x1, local copies, waits for them, and re-layouts  2.02 us

profile of v3, /device:TPU:1, one launch (start us, length us, event | category | flops | bytes accessed | tf_op | source)
XLA Modules:
  0.0 98.8 jit_solution(10826433323845572667)
XLA Ops:
  0.0 96.7 %shard_map.55 = bf16[2048,1024]{1,0:T(8,128)(2,1)S(1)} custom-call(s32[64,128]{1,0:T(8,128)} %bitcast.3, s32[128]{0:T(128)} %pair_map_in.1, s32[64,512]{1,0:T(8,128)} %int_mask_in.1, bf16[32,64,128]{2,1,0:T(8,128)(2,1)} %bitcast.2, bf16[1024,1024]{1,0:T(8,128)(2,1)} %ints.1), custom_call_target="tpu_custom_call" | custom-call | flops 17179869184 | bytes 7340032 | tf_op jit(solution)/shard_map/pallas_call | solution.py:333
  96.7 2.0 %copy.7 = bf16[2048,1024]{1,0:T(8,128)(2,1)} copy(bf16[2048,1024]{1,0:T(8,128)(2,1)S(1)} %shard_map.55) | data formatting | bytes 8388608

commit v4 on v3

--- a/solution.py
+++ b/solution.py
@@ -9,6 +9,7 @@
 HALF = TILE // 2
 MESH = pl.DeviceIdType.MESH
 CHUNKS = 4
+EARLY = 2
 WIDE = 256
 ROWS_STEP = 512
 RINGS = CHUNKS + 10
@@ -65,7 +66,7 @@
 def kernel(
     amp_mask_in, pair_map_in, int_mask_in, amp, ints, out,
     amp_mask, pair_map, int_mask, known_0, known_1, packed_0, packed_1, got_0, got_1,
-    full, ints_in, flag_rows, ints_all, total,
+    full, ints_in, flag_rows, ints_all, early, total,
     ring_send, ring_recv, swap_send, swap_recv, relay_send, relay_recv, local_sem,
 ):
     y = lax.axis_index("row")
@@ -176,6 +177,8 @@
     ring_b[0].start_second()
     for j in range(1, CHUNKS):
         mask_chunk(j)
+    ring_b[0].forward()
+    ring_b[1].start()
     for copy in swap_some:
         copy.wait_recv()
 
@@ -202,17 +205,18 @@
 
     lax.fori_loop(0, 32, choose, 0)
 
-    relays = []
+    relays = {}
 
     def relay(dx, dz, start, size):
         n = len(relays)
+        part = start // 1024
         piece = full.at[place(dx, dz, core), pl.ds(start, size)]
         copy = pltpu.make_async_remote_copy(
             src_ref=piece, dst_ref=piece, send_sem=relay_send.at[n], recv_sem=relay_recv.at[n],
             device_id=twin, device_id_type=MESH,
         )
         copy.start()
-        relays.append(copy)
+        relays[dx, dz, part] = copy
 
     def rows_of(part, half):
         return pl.ds(part * 1024 + half * 512, 512)
@@ -233,8 +237,6 @@
     then_x[0].start()
     first_x.forward()
     first_z.forward()
-    ring_b[0].forward()
-    ring_b[1].start()
     first_x.near()
     first_z.near()
     for d in (-1, 1):
@@ -259,25 +261,63 @@
         if d == -1:
             ring_b[1].forward()
             ring_b[2].start()
+    def lines(m):
+        return pl.ds(pl.multiple_of(m * ROWS_STEP, ROWS_STEP), ROWS_STEP)
+
+    def over_rows(body, start=0, stop=2048):
+        def step(m, carry):
+            body(lines(m))
+            return carry
+
+        lax.fori_loop(start // ROWS_STEP, stop // ROWS_STEP, step, 0)
+
+    def quarter(d):
+        for share in range(2):
+            if share == 0:
+                runs = [(pl.multiple_of((zz * 8 + turn(x, d) * 2) * 128, 256), 2) for zz in range(4)]
+            else:
+                runs = [(pl.multiple_of(turn(z, d) * 1024, 1024), 8)]
+
+            def body(rows):
+                left = jnp.concatenate(
+                    [full[at // 128 + s, rows, :] for at, n in runs for s in range(n)], axis=1
+                )
+                for j in range(EARLY):
+                    right = jnp.concatenate([ints_all[j, pl.ds(at, n * 128), :] for at, n in runs], axis=0)
+                    here = jnp.dot(left, right, preferred_element_type=jnp.float32)
+                    if d != 0:
+                        here = here + early[j, rows, :]
+                    if d != 2:
+                        early[j, rows, :] = here
+                    else:
+                        out[rows, j * WIDE : (j + 1) * WIDE] = here.astype(jnp.bfloat16)
+
+            over_rows(body, share * 1024, (share + 1) * 1024)
+
+    def relayed(d):
+        for e in (0, -1, 1, 2):
+            relays[d, e, 0].wait_recv()
+            if (e, d) != (0, 0):
+                relays[e, d, 1].wait_recv()
+
+    for j in range(EARLY):
+        ring_b[j].near()
+        ring_b[j].far()
+    before = None
     for d in (0, -1, 1, 2):
         then_z[d].far()
         then_x[d].far()
         relay(d, 2, 0, 1024)
         relay(2, d, 1024, 1024)
-    ring_b[2].forward()
-    ring_b[3].start()
-    for copy in relays:
-        copy.wait_recv()
-
-    def lines(m):
-        return pl.ds(pl.multiple_of(m * ROWS_STEP, ROWS_STEP), ROWS_STEP)
-
-    def over_rows(body):
-        def step(m, carry):
-            body(lines(m))
-            return carry
-
-        lax.fori_loop(0, 2048 // ROWS_STEP, step, 0)
+        if d == 0:
+            ring_b[2].forward()
+            ring_b[3].start()
+        else:
+            relayed(before)
+            quarter(before)
+        before = d
+    relayed(before)
+    quarter(before)
 
     def whole(j):
         def body(rows):
@@ -305,15 +345,9 @@
     def end(rows):
         out[rows, last * WIDE : (last + 1) * WIDE] = (total[rows, :] + part(2, rows)).astype(jnp.bfloat16)
 
-    ring_b[0].near()
-    ring_b[0].far()
-    whole(0)
-    ring_b[1].near()
-    ring_b[1].far()
-    whole(1)
-    ring_b[3].forward()
     ring_b[2].near()
     ring_b[2].far()
+    ring_b[3].forward()
     whole(2)
     over_rows(begin)
     ring_b[3].near()
@@ -323,7 +357,7 @@
 
     for each in (*ring_b, first_x, first_z, *then_z.values(), *then_x.values()):
         each.finish()
-    for copy in (*swap_all, *swap_some, *relays):
+    for copy in (*swap_all, *swap_some, *relays.values()):
         copy.wait_send()
 
 
@@ -344,6 +378,7 @@
             pltpu.VMEM((1024, 1024), jnp.bfloat16),
             pltpu.VMEM((16, 1024), jnp.float32),
             pltpu.VMEM((CHUNKS, 4096, WIDE), jnp.bfloat16),
+            pltpu.VMEM((EARLY, 2048, WIDE), jnp.float32),
             pltpu.VMEM((2048, WIDE), jnp.float32),
             pltpu.SemaphoreType.DMA((RINGS, 6)),
             pltpu.SemaphoreType.DMA((RINGS, 6)),

time: 98.8 us -> 94.8 us (0.960)
  Pallas kernels: 96.7 us -> 92.7 us
    pallas_call x1, Pallas kernels: 96.7 us -> 92.7 us  [local(): pl.pallas_call(kernel, out_shape=pltpu.VMEM((2048, 1024), jnp.bfloat16),...]
where the time goes in v4:
time: 94.8 us; the launch traced here: 94.7 us
  Pallas kernels  92.7 us (98%)
  local copies, waits for them, and re-layouts  2.02 us (2%)
    pallas_call x1, Pallas kernels, local(): pl.pallas_call(kernel, out_shape=pltpu.VMEM((2048, 1024), jnp.bfloat16),...  92.7 us
    unnamed x1, local copies, waits for them, and re-layouts  2.02 us

profile of v4, /device:TPU:1, one launch (start us, length us, event | category | flops | bytes accessed | tf_op | source)
XLA Modules:
  0.0 94.7 jit_solution(14381015884044798816)
XLA Ops:
  0.0 92.7 %shard_map.55 = bf16[2048,1024]{1,0:T(8,128)(2,1)S(1)} custom-call(s32[64,128]{1,0:T(8,128)} %bitcast.3, s32[128]{0:T(128)} %pair_map_in.1, s32[64,512]{1,0:T(8,128)} %int_mask_in.1, bf16[32,64,128]{2,1,0:T(8,128)(2,1)} %bitcast.2, bf16[1024,1024]{1,0:T(8,128)(2,1)} %ints.1), custom_call_target="tpu_custom_call" | custom-call | flops 17179869184 | bytes 7340032 | tf_op jit(solution)/shard_map/pallas_call | solution.py:367
  92.7 2.0 %copy.7 = bf16[2048,1024]{1,0:T(8,128)(2,1)} copy(bf16[2048,1024]{1,0:T(8,128)(2,1)S(1)} %shard_map.55) | data formatting | bytes 8388608

commit v5 on v4

--- a/solution.py
+++ b/solution.py
@@ -235,32 +235,6 @@
     relay(0, 0, 0, 2048)
     then_z[0].start()
     then_x[0].start()
-    first_x.forward()
-    first_z.forward()
-    first_x.near()
-    first_z.near()
-    for d in (-1, 1):
-        then_z[d].start()
-        then_x[d].start()
-        relay(d, 0, 0, 1024)
-        relay(0, d, 1024, 1024)
-    first_x.far()
-    first_z.far()
-    then_z[2].start()
-    then_x[2].start()
-    relay(2, 0, 0, 1024)
-    relay(0, 2, 1024, 1024)
-    for d in (0, -1, 1, 2):
-        then_z[d].forward()
-        then_x[d].forward()
-        then_z[d].near()
-        then_x[d].near()
-        for e in (-1, 1):
-            relay(d, e, 0, 1024)
-            relay(e, d, 1024, 1024)
-        if d == -1:
-            ring_b[1].forward()
-            ring_b[2].start()
     def lines(m):
         return pl.ds(pl.multiple_of(m * ROWS_STEP, ROWS_STEP), ROWS_STEP)
 
@@ -300,33 +274,14 @@
             if (e, d) != (0, 0):
                 relays[e, d, 1].wait_recv()
 
-    for j in range(EARLY):
-        ring_b[j].near()
-        ring_b[j].far()
-    before = None
-    for d in (0, -1, 1, 2):
-        then_z[d].far()
-        then_x[d].far()
-        relay(d, 2, 0, 1024)
-        relay(2, d, 1024, 1024)
-        if d == 0:
-            ring_b[2].forward()
-            ring_b[3].start()
-        else:
-            relayed(before)
-            quarter(before)
-        before = d
-    relayed(before)
-    quarter(before)
-
-    def whole(j):
+    def whole(j, start, stop):
         def body(rows):
             left = jnp.concatenate([full[s, rows, :] for s in range(32)], axis=1)
             out[rows, j * WIDE : (j + 1) * WIDE] = jnp.dot(
                 left, ints_all[j], preferred_element_type=jnp.float32
             ).astype(jnp.bfloat16)
 
-        over_rows(body)
+        over_rows(body, start, stop)
 
     last = CHUNKS - 1
 
@@ -345,20 +300,83 @@
     def end(rows):
         out[rows, last * WIDE : (last + 1) * WIDE] = (total[rows, :] + part(2, rows)).astype(jnp.bfloat16)
 
+    def near_two(d):
+        then_z[d].near()
+        then_x[d].near()
+        for e in (-1, 1):
+            relay(d, e, 0, 1024)
+            relay(e, d, 1024, 1024)
+
+    def far_two(d):
+        then_z[d].far()
+        then_x[d].far()
+        relay(d, 2, 0, 1024)
+        relay(2, d, 1024, 1024)
+
+    def forward_two(d):
+        then_z[d].forward()
+        then_x[d].forward()
+
+    def start_two(d):
+        then_z[d].start()
+        then_x[d].start()
+
+    first_x.forward()
+    first_z.forward()
+    first_x.near()
+    first_z.near()
+    start_two(-1)
+    for d in (-1, 1):
+        relay(d, 0, 0, 1024)
+        relay(0, d, 1024, 1024)
+    forward_two(0)
+    start_two(1)
+    near_two(0)
+    first_x.far()
+    first_z.far()
+    relay(2, 0, 0, 1024)
+    relay(0, 2, 1024, 1024)
+    ring_b[1].forward()
+    ring_b[2].start()
+    forward_two(-1)
+    start_two(2)
+    near_two(-1)
+    far_two(0)
+    for j in range(EARLY):
+        ring_b[j].near()
+        ring_b[j].far()
+    forward_two(1)
+    relayed(0)
+    quarter(0)
+    near_two(1)
+    far_two(-1)
+    ring_b[2].forward()
+    ring_b[3].start()
+    relayed(-1)
+    quarter(-1)
+    forward_two(2)
+    near_two(2)
+    far_two(1)
+    relayed(1)
+    quarter(1)
+    far_two(2)
     ring_b[2].near()
     ring_b[2].far()
+    relayed(2)
+    quarter(2)
+    whole(2, 0, 1024)
     ring_b[3].forward()
-    whole(2)
+    whole(2, 1024, 2048)
     over_rows(begin)
+    for each in (*ring_b[:3], first_x, first_z, *then_z.values(), *then_x.values()):
+        each.finish()
+    for copy in (*swap_all, *swap_some, *relays.values()):
+        copy.wait_send()
     ring_b[3].near()
     over_rows(add)
     ring_b[3].far()
     over_rows(end)
-
-    for each in (*ring_b, first_x, first_z, *then_z.values(), *then_x.values()):
-        each.finish()
-    for copy in (*swap_all, *swap_some, *relays.values()):
-        copy.wait_send()
+    ring_b[3].finish()
 
 
 def local(amplitudes, integrals, amp_mask, int_mask, pair_map):

time: 94.8 us -> 93.9 us (level)
  no operation moved by 1% of the time
where the time goes in v5:
time: 93.9 us; the launch traced here: 93.8 us
  Pallas kernels  91.8 us (98%)
  local copies, waits for them, and re-layouts  2.02 us (2%)
    pallas_call x1, Pallas kernels, local(): pl.pallas_call(kernel, out_shape=pltpu.VMEM((2048, 1024), jnp.bfloat16),...  91.8 us
    unnamed x1, local copies, waits for them, and re-layouts  2.02 us

profile of v5, /device:TPU:1, one launch (start us, length us, event | category | flops | bytes accessed | tf_op | source)
XLA Modules:
  0.0 93.8 jit_solution(9038077354313702996)
XLA Ops:
  0.0 91.8 %shard_map.55 = bf16[2048,1024]{1,0:T(8,128)(2,1)S(1)} custom-call(s32[64,128]{1,0:T(8,128)} %bitcast.3, s32[128]{0:T(128)} %pair_map_in.1, s32[64,512]{1,0:T(8,128)} %int_mask_in.1, bf16[32,64,128]{2,1,0:T(8,128)(2,1)} %bitcast.2, bf16[1024,1024]{1,0:T(8,128)(2,1)} %ints.1), custom_call_target="tpu_custom_call" | custom-call | flops 17179869184 | bytes 7340032 | tf_op jit(solution)/shard_map/pallas_call | solution.py:385
  91.8 2.0 %copy.7 = bf16[2048,1024]{1,0:T(8,128)(2,1)} copy(bf16[2048,1024]{1,0:T(8,128)(2,1)S(1)} %shard_map.55) | data formatting | bytes 8388608

commit v6 on v5

--- a/solution.py
+++ b/solution.py
@@ -11,7 +11,9 @@
 CHUNKS = 4
 EARLY = 2
 WIDE = 256
-ROWS_STEP = 512
+WHOLE_STEP = 512
+PART_STEP = 1024
+LAST_STEP = 2048
 RINGS = CHUNKS + 10
 RELAYS = 31
 
@@ -235,15 +237,12 @@
     relay(0, 0, 0, 2048)
     then_z[0].start()
     then_x[0].start()
-    def lines(m):
-        return pl.ds(pl.multiple_of(m * ROWS_STEP, ROWS_STEP), ROWS_STEP)
-
-    def over_rows(body, start=0, stop=2048):
+    def over_rows(body, size, start=0, stop=2048):
         def step(m, carry):
-            body(lines(m))
+            body(pl.ds(pl.multiple_of(m * size, size), size))
             return carry
 
-        lax.fori_loop(start // ROWS_STEP, stop // ROWS_STEP, step, 0)
+        lax.fori_loop(start // size, stop // size, step, 0)
 
     def quarter(d):
         for share in range(2):
@@ -266,7 +265,7 @@
                     else:
                         out[rows, j * WIDE : (j + 1) * WIDE] = here.astype(jnp.bfloat16)
 
-            over_rows(body, share * 1024, (share + 1) * 1024)
+            over_rows(body, PART_STEP, share * 1024, (share + 1) * 1024)
 
     def relayed(d):
         for e in (0, -1, 1, 2):
@@ -281,24 +280,26 @@
                 left, ints_all[j], preferred_element_type=jnp.float32
             ).astype(jnp.bfloat16)
 
-        over_rows(body, start, stop)
+        over_rows(body, WHOLE_STEP, start, stop)
 
     last = CHUNKS - 1
 
-    def part(d, rows):
-        plane = turn(y, d)
-        left = jnp.concatenate([full[plane * 8 + s, rows, :] for s in range(8)], axis=1)
-        right = ints_all[last, pl.ds(pl.multiple_of(plane * 1024, 1024), 1024), :]
+    def part(rows, *planes):
+        starts = [turn(y, d) * 8 for d in planes]
+        left = jnp.concatenate([full[start + s, rows, :] for start in starts for s in range(8)], axis=1)
+        right = jnp.concatenate(
+            [ints_all[last, pl.ds(pl.multiple_of(start * 128, 1024), 1024), :] for start in starts], axis=0
+        )
         return jnp.dot(left, right, preferred_element_type=jnp.float32)
 
     def begin(rows):
-        total[rows, :] = part(0, rows)
+        total[rows, :] = part(rows, 0)
 
     def add(rows):
-        total[rows, :] += part(-1, rows) + part(1, rows)
+        total[rows, :] += part(rows, -1, 1)
 
     def end(rows):
-        out[rows, last * WIDE : (last + 1) * WIDE] = (total[rows, :] + part(2, rows)).astype(jnp.bfloat16)
+        out[rows, last * WIDE : (last + 1) * WIDE] = (total[rows, :] + part(rows, 2)).astype(jnp.bfloat16)
 
     def near_two(d):
         then_z[d].near()
@@ -367,15 +368,15 @@
     whole(2, 0, 1024)
     ring_b[3].forward()
     whole(2, 1024, 2048)
-    over_rows(begin)
+    over_rows(begin, PART_STEP)
     for each in (*ring_b[:3], first_x, first_z, *then_z.values(), *then_x.values()):
         each.finish()
     for copy in (*swap_all, *swap_some, *relays.values()):
         copy.wait_send()
     ring_b[3].near()
-    over_rows(add)
+    over_rows(add, PART_STEP)
     ring_b[3].far()
-    over_rows(end)
+    over_rows(end, LAST_STEP)
     ring_b[3].finish()
 
 

time: 93.9 us -> 92 us (0.980)
  Pallas kernels: 91.8 us -> 89.9 us
    pallas_call x1, Pallas kernels: 91.8 us -> 89.9 us  [local(): pl.pallas_call(kernel, out_shape=pltpu.VMEM((2048, 1024), jnp.bfloat16),...]
where the time goes in v6:
time: 92 us; the launch traced here: 91.9 us
  Pallas kernels  89.9 us (98%)
  local copies, waits for them, and re-layouts  2.02 us (2%)
    pallas_call x1, Pallas kernels, local(): pl.pallas_call(kernel, out_shape=pltpu.VMEM((2048, 1024), jnp.bfloat16),...  89.9 us
    unnamed x1, local copies, waits for them, and re-layouts  2.02 us

profile of v6, /device:TPU:1, one launch (start us, length us, event | category | flops | bytes accessed | tf_op | source)
XLA Modules:
  0.0 91.9 jit_solution(6604673089700611487)
XLA Ops:
  0.0 89.9 %shard_map.55 = bf16[2048,1024]{1,0:T(8,128)(2,1)S(1)} custom-call(s32[64,128]{1,0:T(8,128)} %bitcast.3, s32[128]{0:T(128)} %pair_map_in.1, s32[64,512]{1,0:T(8,128)} %int_mask_in.1, bf16[32,64,128]{2,1,0:T(8,128)(2,1)} %bitcast.2, bf16[1024,1024]{1,0:T(8,128)(2,1)} %ints.1), custom_call_target="tpu_custom_call" | custom-call | flops 17179869184 | bytes 7340032 | tf_op jit(solution)/shard_map/pallas_call | solution.py:386
  89.9 2.0 %copy.7 = bf16[2048,1024]{1,0:T(8,128)(2,1)} copy(bf16[2048,1024]{1,0:T(8,128)(2,1)S(1)} %shard_map.55) | data formatting | bytes 8388608

commit v7 on v6

--- a/solution.py
+++ b/solution.py
@@ -14,6 +14,7 @@
 WHOLE_STEP = 512
 PART_STEP = 1024
 LAST_STEP = 2048
+WRITES = 8
 RINGS = CHUNKS + 10
 RELAYS = 31
 
@@ -380,10 +381,22 @@
     ring_b[3].finish()
 
 
+def write(result, out, sems):
+    size = 2048 // WRITES
+    copies = [
+        pltpu.make_async_copy(result.at[pl.ds(i * size, size)], out.at[pl.ds(i * size, size)], sems.at[i])
+        for i in range(WRITES)
+    ]
+    for copy in copies:
+        copy.start()
+    for copy in copies:
+        copy.wait()
+
+
 def local(amplitudes, integrals, amp_mask, int_mask, pair_map):
     anywhere = pl.BlockSpec(memory_space=pl.ANY)
     half_tiles = [pltpu.VMEM((n, HALF, 128), jnp.bfloat16) for n in (64, 64, 32, 32, 32, 32)]
-    return pl.pallas_call(
+    result = pl.pallas_call(
         kernel,
         out_shape=pltpu.VMEM((2048, 1024), jnp.bfloat16),
         in_specs=[anywhere] * 5,
@@ -412,6 +425,13 @@
         ),
         cost_estimate=pl.CostEstimate(flops=2 * 2048 * 4096 * 1024, bytes_accessed=7 * 2**20, transcendentals=0),
     )(amp_mask.T, pair_map, int_mask, amplitudes.reshape(32, TILE, 128), integrals)
+    return pl.pallas_call(
+        write,
+        out_shape=jax.ShapeDtypeStruct((2048, 1024), jnp.bfloat16),
+        in_specs=[pl.BlockSpec(memory_space=pltpu.VMEM)],
+        out_specs=anywhere,
+        scratch_shapes=[pltpu.SemaphoreType.DMA((WRITES,))],
+    )(result)
 
 
 def solution(mesh):

time: 92 us -> 96.2 us (1.046)
  Pallas kernels: 89.9 us -> 94.2 us
    pallas_call x0 -> x1, Pallas kernels: none -> 4.25 us  [local(): pl.pallas_call(write, out_shape=jax.ShapeDtypeStruct((2048, 1024), jnp.bf...]
    unnamed x1 -> x2, local copies, waits for them, and re-layouts: 2.02 us -> 1.93 us
where the time goes in v7:
time: 96.2 us; the launch traced here: 96.1 us
  Pallas kernels  94.2 us (98%)
  local copies, waits for them, and re-layouts  1.93 us (2%)
    pallas_call x1, Pallas kernels, local(): pl.pallas_call(kernel, out_shape=pltpu.VMEM((2048, 1024), jnp.bfloat16),...  89.9 us
    pallas_call x1, Pallas kernels, local(): pl.pallas_call(write, out_shape=jax.ShapeDtypeStruct((2048, 1024), jnp.bf...  4.25 us
    unnamed x2, local copies, waits for them, and re-layouts  1.93 us

profile of v7, /device:TPU:1, one launch (start us, length us, event | category | flops | bytes accessed | tf_op | source)
XLA Modules:
  0.0 96.1 jit_solution(1847099251443703491)
XLA Ops:
  0.0 89.9 %shard_map.55.result = bf16[2048,1024]{1,0:T(8,128)(2,1)S(1)} custom-call(s32[64,128]{1,0:T(8,128)} %bitcast.3, s32[128]{0:T(128)} %pair_map_in.1, s32[64,512]{1,0:T(8,128)} %int_mask_in.1, bf16[32,64,128]{2,1,0:T(8,128)(2,1)} %bitcast.2, bf16[1024,1024]{1,0:T(8,128)(2,1)} %ints.1), custom_call_target="tpu_custom_call" | custom-call | flops 17179869184 | bytes 7340032 | tf_op jit(solution)/shard_map/pallas_call | solution.py:399
  89.9 0.0 copy-start
  89.9 1.9 %copy-done = bf16[2048,1024]{1,0:T(8,128)(2,1)} copy-done((bf16[2048,1024]{1,0:T(8,128)(2,1)}, bf16[2048,1024]{1,0:T(8,128)(2,1)S(1)}, u32[]{:S(2)}) %copy-start) | copy-done | bytes 4194328
  91.8 4.3 %shard_map.56 = bf16[2048,1024]{1,0:T(8,128)(2,1)} custom-call(bf16[2048,1024]{1,0:T(8,128)(2,1)} %copy-done), custom_call_target="tpu_custom_call" | custom-call | tf_op jit(solution)/shard_map/pallas_call | solution.py:428
Async XLA Ops:
  89.9 1.9 %copy-start = (bf16[2048,1024]{1,0:T(8,128)(2,1)}, bf16[2048,1024]{1,0:T(8,128)(2,1)S(1)}, u32[]{:S(2)}) copy-start(bf16[2048,1024]{1,0:T(8,128)(2,1)S(1)} %shard_map.55.result) | copy-start | bytes 12582916

commit v8 on v6

--- a/solution.py
+++ b/solution.py
@@ -107,7 +107,7 @@
         pltpu.make_async_copy(half_rows(0), known_0.at[pl.ds(0, 32)], local_sem.at[4]),
         pltpu.make_async_copy(half_rows(1), known_1.at[pl.ds(0, 32)], local_sem.at[5]),
     ]
-    for copy in (int_mask_copy, ints_copy, *amp_copies):
+    for copy in (*amp_copies[2:], int_mask_copy, ints_copy, *amp_copies[:2]):
         copy.start()
 
     odd = lax.rem(y, 2)
@@ -121,12 +121,13 @@
             device_id=(to, col), device_id_type=MESH,
         )
 
-    swap_all = [swap(h, half_rows(h), known[h].at[pl.ds(32, 32)], first[h]) for h in (0, 1)]
+    swap_all = [swap(h, known[h].at[pl.ds(0, 32)], known[h].at[pl.ds(32, 32)], first[h]) for h in (0, 1)]
     swap_some = [swap(2 + h, packed[h], got[h], second[h]) for h in (0, 1)]
 
     pl.semaphore_wait(barrier, 7)
-    for copy in swap_all:
-        copy.start()
+    for h in (0, 1):
+        amp_copies[2 + h].wait()
+        swap_all[h].start()
 
     wide = CHUNKS * WIDE
     chosen = lax.broadcasted_iota(jnp.int32, (512, wide), 0)
@@ -162,7 +163,7 @@
     mask_chunk(0)
     ring_b[0].start_first()
 
-    for copy in amp_copies:
+    for copy in amp_copies[:2]:
         copy.wait()
     for h in (0, 1):
         swap_all[h].wait_recv()

time: 92 us -> 91.8 us (level)
  no operation moved by 1% of the time
where the time goes in v8:
time: 91.8 us; the launch traced here: 91.7 us
  Pallas kernels  89.7 us (98%)
  local copies, waits for them, and re-layouts  2.02 us (2%)
    pallas_call x1, Pallas kernels, local(): pl.pallas_call(kernel, out_shape=pltpu.VMEM((2048, 1024), jnp.bfloat16),...  89.7 us
    unnamed x1, local copies, waits for them, and re-layouts  2.02 us

profile of v8, /device:TPU:1, one launch (start us, length us, event | category | flops | bytes accessed | tf_op | source)
XLA Modules:
  0.0 91.7 jit_solution(3230504369672924257)
XLA Ops:
  0.0 89.7 %shard_map.55 = bf16[2048,1024]{1,0:T(8,128)(2,1)S(1)} custom-call(s32[64,128]{1,0:T(8,128)} %bitcast.3, s32[128]{0:T(128)} %pair_map_in.1, s32[64,512]{1,0:T(8,128)} %int_mask_in.1, bf16[32,64,128]{2,1,0:T(8,128)(2,1)} %bitcast.2, bf16[1024,1024]{1,0:T(8,128)(2,1)} %ints.1), custom_call_target="tpu_custom_call" | custom-call | flops 17179869184 | bytes 7340032 | tf_op jit(solution)/shard_map/pallas_call | solution.py:387
  89.7 2.0 %copy.7 = bf16[2048,1024]{1,0:T(8,128)(2,1)} copy(bf16[2048,1024]{1,0:T(8,128)(2,1)S(1)} %shard_map.55) | data formatting | bytes 8388608
